TPU v7x, 32 devices: a whole 2x2x4 slice. The times are simulated.
32 devices in a mesh: region: 32 (over z, y, x, core).
Axes of the slice: x: 2, y: 2, z: 4, core: 2. Of those that a mesh axis runs over, the one named last changes fastest.
Arguments:
- node_feat: bfloat16 [16384, 512], P('region'), may hold values from -6 to 6
- edge_feat: bfloat16 [131072, 512], P('region'), may hold values from -6 to 6
- sender: int32 [131072], P('region'), may hold values from 0 to 1279, as said below
- receiver: int32 [131072], P('region'), may hold values from 0 to 512, as said below
- send_list: int32 [32, 8, 32], P('region'), may hold values from 16 to 511
- edge_w1: bfloat16 [1536, 512], replicated, may hold values from -0.15625 to 0.15625
- edge_b1: float32 [512], replicated, may hold values from -4 to 4
- edge_w2: bfloat16 [512, 512], replicated, may hold values from -0.25 to 0.25
- edge_b2: float32 [512], replicated, may hold values from -4 to 4
- edge_gain: float32 [512], replicated, may hold values from 0.5 to 1.5
- edge_shift: float32 [512], replicated, may hold values from -4 to 4
- node_w1: bfloat16 [1024, 512], replicated, may hold values from -0.1875 to 0.1875
- node_b1: float32 [512], replicated, may hold values from -4 to 4
- node_w2: bfloat16 [512, 512], replicated, may hold values from -0.25 to 0.25
- node_b2: float32 [512], replicated, may hold values from -4 to 4
- node_gain: float32 [512], replicated, may hold values from 0.5 to 1.5
- node_shift: float32 [512], replicated, may hold values from -4 to 4
Outputs:
- edge_out: bfloat16 [131072, 512], P('region')
- node_out: bfloat16 [16384, 512], P('region')
Inputs may be any that keep to these rules, and one draw needn't show every extreme that they name: `sender`: a row of the region's table as built in the first step; every region has slots pointing at row 0 and at the last row. `receiver`: non-decreasing within each region's 4096 slots; the value 512 marks an empty slot, and empty slots stand after the used ones; some region uses all its slots. `send_list`: entry [s, j, k] is a local index on region s of a node that s sends to its j-th neighbour.
All inputs are finite; a program needn't handle non-finite values.
Results may differ from a plain program's by a relative error of at most 0.0043.
Values may be sent and summed in bfloat16 or wider, within the bound.
A program may use at most 128 MiB of HBM per device.

v0:
```python
import jax
import jax.numpy as jnp
from jax import lax
from jax.sharding import PartitionSpec as P

COARSE_DEV = 16


NEIGHBOUR_STEPS = (1, -1, 7, -7, 8, -8, 9, -9)


def from_behind(block, axis, distance):
    devices = range(lax.axis_size(axis))
    route = [((i - distance) % len(devices), i) for i in devices]
    return lax.ppermute(block, axis, route)


def finish(pre, w_second, b_second, gain, shift):
    hidden = jax.nn.silu(pre).astype(jnp.bfloat16)
    out = jnp.dot(hidden, w_second, preferred_element_type=jnp.float32) + b_second
    mean = jnp.mean(out, axis=-1, keepdims=True)
    var = jnp.mean((out - mean) ** 2, axis=-1, keepdims=True)
    return (out - mean) * lax.rsqrt(var + 1e-05) * gain + shift


def pick_rows(wanted_rows, source, block_size):
    total_rows = wanted_rows.shape[0]
    grouped = wanted_rows.reshape(total_rows // block_size, block_size)
    source_ids = jnp.arange(source.shape[0], dtype=jnp.int32)

    def select(group_rows):
        one_hot = (group_rows[:, None] == source_ids[None, :]).astype(source.dtype)
        return jnp.dot(one_hot, source, preferred_element_type=jnp.float32).astype(source.dtype)

    return lax.map(select, grouped).reshape(total_rows, source.shape[1])


def on_device(
    node_feat,
    edge_feat,
    sender,
    receiver,
    send_list,
    edge_w1,
    edge_b1,
    edge_w2,
    edge_b2,
    edge_gain,
    edge_shift,
    node_w1,
    node_b1,
    node_w2,
    node_b2,
    node_gain,
    node_shift,
):
    width = node_feat.shape[1]
    node_rows = node_feat.shape[0]
    edge_rows = edge_feat.shape[0]
    neighbours = send_list.shape[1]
    slots = send_list.shape[2]
    block_size = min(512, edge_rows)
    block_count = edge_rows // block_size
    coarse = node_feat[:COARSE_DEV]
    outgoing = jnp.take(node_feat, send_list[0].reshape(-1), axis=0).reshape(
        neighbours, slots, width
    )
    coarse_all = lax.all_gather(coarse, "region", axis=0, tiled=True)
    arrived = [
        from_behind(rows_out, "region", distance)
        for rows_out, distance in zip(list(outgoing), NEIGHBOUR_STEPS)
    ]
    halo = jnp.concatenate(arrived, axis=0)
    table = jnp.concatenate([node_feat, coarse_all, halo], axis=0)
    live = receiver < node_rows
    recv_index = jnp.minimum(receiver, node_rows - 1)
    sent_rows = pick_rows(sender, table, block_size)
    recv_rows = pick_rows(recv_index, node_feat, block_size)
    inputs = jnp.concatenate([edge_feat, sent_rows, recv_rows], axis=1)
    edge_pre = jnp.dot(inputs, edge_w1, preferred_element_type=jnp.float32) + edge_b1
    update = finish(edge_pre, edge_w2, edge_b2, edge_gain, edge_shift)
    edge_out = jnp.where(live[:, None], edge_feat.astype(jnp.float32) + update, 0.0).astype(
        jnp.bfloat16
    )
    node_ids = jnp.arange(node_rows, dtype=jnp.int32)

    def add_block(position, running):
        first_slot = position * block_size
        block_rows = lax.dynamic_slice_in_dim(edge_out, first_slot, block_size, 0)
        block_ids = lax.dynamic_slice_in_dim(receiver, first_slot, block_size, 0)
        one_hot = (node_ids[:, None] == block_ids[None, :]).astype(jnp.bfloat16)
        return running + jnp.dot(one_hot, block_rows, preferred_element_type=jnp.float32)

    summed = lax.fori_loop(0, block_count, add_block, jnp.zeros((node_rows, width), jnp.float32))
    aggregate = summed.astype(jnp.bfloat16)
    node_in = jnp.concatenate([node_feat, aggregate], axis=1)
    node_pre = jnp.dot(node_in, node_w1, preferred_element_type=jnp.float32) + node_b1
    node_update = finish(node_pre, node_w2, node_b2, node_gain, node_shift)
    node_out = (node_feat.astype(jnp.float32) + node_update).astype(jnp.bfloat16)
    return (edge_out, node_out)


def solution(mesh):
    in_specs = (
        P("region", None),
        P("region", None),
        P("region"),
        P("region"),
        P("region", None, None),
        P(),
        P(),
        P(),
        P(),
        P(),
        P(),
        P(),
        P(),
        P(),
        P(),
        P(),
        P(),
    )
    out_specs = (P("region", None), P("region", None))
    return jax.shard_map(
        on_device, mesh=mesh, in_specs=in_specs, out_specs=out_specs, check_vma=False
    )
```

profile of v0, /device:TPU:0, one launch (start us, length us, event | category | flops | bytes accessed | tf_op | source)
XLA Modules:
  0.0 168.2 jit_solution(16734785573376712712)
XLA Ops:
  0.7 0.9 reshape_squeeze.6
  1.6 0.8 reshape_squeeze.5
  2.4 2.4 %gather_fusion = bf16[256,512]{1,0:T(8,128)(2,1)S(1)} fusion(bf16[512,512]{1,0:T(8,128)(2,1)} %param.23, s32[1024]{0:T(1024)S(1)} %pad_clamp_fusion), kind=kCustom, calls=%fused_computation | custom fusion | bytes 525312 | tf_op jit(solution)/shard_map/jit(_take)/gather | solution.py:65
  4.7 0.1 broadcast_select_fusion
  4.9 0.5 collective-permute-start
  5.4 6.0 %collective-permute-start.1 = (bf16[32,512]{1,0:T(8,128)(2,1)S(1)}, bf16[32,512]{1,0:T(8,128)(2,1)}, u32[]{:S(2)}, u32[]{:S(2)}) collective-permute-start(bf16[32,512]{1,0:T(8,128)(2,1)S(1)} %get-tuple-element.226), channel_id=1, source_target_pairs={{1,0},{2,1},{3,2},{4,3},{5,4},{6,5},{7,6},{8,7},{9,8},{10,9},{11,1... | collective-permute-start | bytes 98312 | tf_op jit(solution)/shard_map/ppermute | solution.py:15
  11.4 3.5 %collective-permute-start.3 = (bf16[32,512]{1,0:T(8,128)(2,1)S(1)}, bf16[32,512]{1,0:T(8,128)(2,1)S(1)}, u32[]{:S(2)}, u32[]{:S(2)}) collective-permute-start(bf16[32,512]{1,0:T(8,128)(2,1)S(1)} %get-tuple-element.224), channel_id=1, source_target_pairs={{7,0},{8,1},{9,2},{10,3},{11,4},{12,5},{13,6},{14,7},{15,8},{16,9}... | collective-permute-start | bytes 98312 | tf_op jit(solution)/shard_map/ppermute | solution.py:15
  14.9 1.9 %constant_dynamic-update-slice_fusion.9 = bf16[1280,512]{1,0:T(8,128)(2,1)} fusion(bf16[512,512]{1,0:T(8,128)(2,1)} %param.23), kind=kLoop, calls=%fused_computation.55 | loop fusion | bytes 1048576
  16.8 0.6 broadcast_compare_fusion
  17.4 40.1 %all_gather.3 = bf16[512,512]{1,0:T(8,128)(2,1)S(1)} all-gather(bf16[16,512]{1,0:T(8,128)(2,1)S(1)} %slice-done), channel_id=1, replica_groups=mesh['region'=32] {'region'}, dimensions={0}, use_global_device_ids=true | all-gather | bytes 540672 | tf_op jit(solution)/shard_map/all_gather | solution.py:68
  57.6 2.3 %broadcast.84.clone = bf16[8,512,512]{2,1,0:T(8,128)(2,1)} broadcast(bf16[]{:T(256)} %constant.76.clone.1), dimensions={} | broadcast | bytes 4194306 | tf_op jit(solution)/shard_map/broadcast.9
  59.9 10.5 %while.37 = (s32[]{:T(128)}, bf16[8,512,512]{2,1,0:T(8,128)(2,1)}, s32[8,512]{1,0:T(8,128)S(1)}, bf16[512,512]{1,0:T(8,128)(2,1)S(1)}, s32[]{:T(128)}) while((s32[]{:T(128)}, bf16[8,512,512]{2,1,0:T(8,128)(2,1)}, s32[8,512]{1,0:T(8,128)S(1)}, bf16[512,512]{1,0:T(8,128)(2,1)S(1)}, s32[]{:T(128)}) %tuple.88), condition=%wide.region_3.4_spmd.clone, body=%wide.region_2.3_spmd.clone.sunk | while | flops 268959744 | bytes 1055297 | solution.py:35
  59.9 1.3 fusion.65
  61.2 1.3 fusion.65
  62.5 1.3 fusion.65
  63.8 1.3 fusion.65
  65.1 1.3 fusion.65
  66.4 1.3 fusion.65
  67.7 1.3 fusion.65
  69.1 1.3 fusion.65
  70.4 0.8 constant_dynamic-update-slice_fusion.8
  71.2 1.0 copy.20
  72.2 6.3 %copy.19 = bf16[4096,512]{0,1:T(8,128)(2,1)} copy(bf16[4096,512]{1,0:T(8,128)(2,1)} %param.24) | data formatting | bytes 8388608 | tf_op args[1]
  78.5 1.4 constant_dynamic-update-slice_fusion.7
  79.9 1.7 %collective-permute-start.6 = (bf16[32,512]{1,0:T(8,128)(2,1)S(1)}, bf16[32,512]{1,0:T(8,128)(2,1)S(1)}, u32[]{:S(2)}, u32[]{:S(2)}) collective-permute-start(bf16[32,512]{1,0:T(8,128)(2,1)S(1)} %get-tuple-element.221), channel_id=1, source_target_pairs={{23,0},{24,1},{25,2},{26,3},{27,4},{28,5},{29,6},{30,7},{31,8},{0,... | collective-permute-start | bytes 98312 | tf_op jit(solution)/shard_map/ppermute | solution.py:15
  81.6 1.4 constant_dynamic-update-slice_fusion.6
  83.0 2.7 %collective-permute-start.7 = (bf16[32,512]{1,0:T(8,128)(2,1)S(1)}, bf16[32,512]{1,0:T(8,128)(2,1)S(1)}, u32[]{:S(2)}, u32[]{:S(2)}) collective-permute-start(bf16[32,512]{1,0:T(8,128)(2,1)S(1)} %get-tuple-element.220), channel_id=1, source_target_pairs={{9,0},{10,1},{11,2},{12,3},{13,4},{14,5},{15,6},{16,7},{17,8},{18,... | collective-permute-start | bytes 98312 | tf_op jit(solution)/shard_map/ppermute | solution.py:15
  85.7 0.6 constant_dynamic-update-slice_fusion.5
  86.3 0.6 constant_dynamic-update-slice_fusion.4
  87.0 0.6 constant_dynamic-update-slice_fusion.3
  87.6 0.6 constant_dynamic-update-slice_fusion.2
  88.2 0.6 constant_dynamic-update-slice_fusion.1
  88.8 0.6 constant_dynamic-update-slice_fusion
  89.4 2.3 %broadcast.84.clone.1 = bf16[8,512,512]{2,1,0:T(8,128)(2,1)} broadcast(bf16[]{:T(256)} %constant.76.clone.1), dimensions={} | broadcast | bytes 4194306 | tf_op jit(solution)/shard_map/broadcast.9
  91.8 24.2 %while.36 = (s32[]{:T(128)}, bf16[8,512,512]{2,1,0:T(8,128)(2,1)}, s32[8,512]{1,0:T(8,128)S(1)}, bf16[1280,512]{1,0:T(8,128)(2,1)}, s32[]{:T(128)}) while((s32[]{:T(128)}, bf16[8,512,512]{2,1,0:T(8,128)(2,1)}, s32[8,512]{1,0:T(8,128)S(1)}, bf16[1280,512]{1,0:T(8,128)(2,1)}, s32[]{:T(128)}) %tuple.82), condition=%wide.region_1.2_spmd.clone, body=%wide.region_0.1_spmd.clone.sunk | while | flops 672006144 | bytes 1841729 | solution.py:35
  91.8 3.1 %fusion.63 = bf16[8,512,512]{2,1,0:T(8,128)(2,1)} fusion(bf16[8,512,512]{2,1,0:T(8,128)(2,1)} %get-tuple-element.328, s32[]{:T(128)} %get-tuple-element.327, bf16[1280,512]{1,0:T(8,128)(2,1)} %get-tuple-element.335, s32[512]{0:T(512)S(1)} %bitcast.34), kind=kOutput, calls=%fused_computation.9.clone.1 | convolution fusion | flops 672006144 | bytes 1837568 | tf_op jit(solution)/shard_map/while/body/eval_jaxpr/dot_general | solution.py:33
  94.8 3.0 %fusion.63 = bf16[8,512,512]{2,1,0:T(8,128)(2,1)} fusion(bf16[8,512,512]{2,1,0:T(8,128)(2,1)} %get-tuple-element.328, s32[]{:T(128)} %get-tuple-element.327, bf16[1280,512]{1,0:T(8,128)(2,1)} %get-tuple-element.335, s32[512]{0:T(512)S(1)} %bitcast.34), kind=kOutput, calls=%fused_computation.9.clone.1 | convolution fusion | flops 672006144 | bytes 1837568 | tf_op jit(solution)/shard_map/while/body/eval_jaxpr/dot_general | solution.py:33
  97.9 3.0 %fusion.63 = bf16[8,512,512]{2,1,0:T(8,128)(2,1)} fusion(bf16[8,512,512]{2,1,0:T(8,128)(2,1)} %get-tuple-element.328, s32[]{:T(128)} %get-tuple-element.327, bf16[1280,512]{1,0:T(8,128)(2,1)} %get-tuple-element.335, s32[512]{0:T(512)S(1)} %bitcast.34), kind=kOutput, calls=%fused_computation.9.clone.1 | convolution fusion | flops 672006144 | bytes 1837568 | tf_op jit(solution)/shard_map/while/body/eval_jaxpr/dot_general | solution.py:33
  100.9 3.0 %fusion.63 = bf16[8,512,512]{2,1,0:T(8,128)(2,1)} fusion(bf16[8,512,512]{2,1,0:T(8,128)(2,1)} %get-tuple-element.328, s32[]{:T(128)} %get-tuple-element.327, bf16[1280,512]{1,0:T(8,128)(2,1)} %get-tuple-element.335, s32[512]{0:T(512)S(1)} %bitcast.34), kind=kOutput, calls=%fused_computation.9.clone.1 | convolution fusion | flops 672006144 | bytes 1837568 | tf_op jit(solution)/shard_map/while/body/eval_jaxpr/dot_general | solution.py:33
  103.9 3.0 %fusion.63 = bf16[8,512,512]{2,1,0:T(8,128)(2,1)} fusion(bf16[8,512,512]{2,1,0:T(8,128)(2,1)} %get-tuple-element.328, s32[]{:T(128)} %get-tuple-element.327, bf16[1280,512]{1,0:T(8,128)(2,1)} %get-tuple-element.335, s32[512]{0:T(512)S(1)} %bitcast.34), kind=kOutput, calls=%fused_computation.9.clone.1 | convolution fusion | flops 672006144 | bytes 1837568 | tf_op jit(solution)/shard_map/while/body/eval_jaxpr/dot_general | solution.py:33
  106.9 3.0 %fusion.63 = bf16[8,512,512]{2,1,0:T(8,128)(2,1)} fusion(bf16[8,512,512]{2,1,0:T(8,128)(2,1)} %get-tuple-element.328, s32[]{:T(128)} %get-tuple-element.327, bf16[1280,512]{1,0:T(8,128)(2,1)} %get-tuple-element.335, s32[512]{0:T(512)S(1)} %bitcast.34), kind=kOutput, calls=%fused_computation.9.clone.1 | convolution fusion | flops 672006144 | bytes 1837568 | tf_op jit(solution)/shard_map/while/body/eval_jaxpr/dot_general | solution.py:33
  109.9 3.0 %fusion.63 = bf16[8,512,512]{2,1,0:T(8,128)(2,1)} fusion(bf16[8,512,512]{2,1,0:T(8,128)(2,1)} %get-tuple-element.328, s32[]{:T(128)} %get-tuple-element.327, bf16[1280,512]{1,0:T(8,128)(2,1)} %get-tuple-element.335, s32[512]{0:T(512)S(1)} %bitcast.34), kind=kOutput, calls=%fused_computation.9.clone.1 | convolution fusion | flops 672006144 | bytes 1837568 | tf_op jit(solution)/shard_map/while/body/eval_jaxpr/dot_general | solution.py:33
  112.9 3.0 %fusion.63 = bf16[8,512,512]{2,1,0:T(8,128)(2,1)} fusion(bf16[8,512,512]{2,1,0:T(8,128)(2,1)} %get-tuple-element.328, s32[]{:T(128)} %get-tuple-element.327, bf16[1280,512]{1,0:T(8,128)(2,1)} %get-tuple-element.335, s32[512]{0:T(512)S(1)} %bitcast.34), kind=kOutput, calls=%fused_computation.9.clone.1 | convolution fusion | flops 672006144 | bytes 1837568 | tf_op jit(solution)/shard_map/while/body/eval_jaxpr/dot_general | solution.py:33
  116.0 13.9 %add_reduce_fusion = (f32[4096]{0:T(1024)S(1)}, f32[4096,512]{0,1:T(8,128)}) fusion(f32[512]{0:T(512)S(1)} %copy-done.6, bf16[512,512]{1,0:T(8,128)(2,1)} %param.30, bf16[1536,512]{1,0:T(8,128)(2,1)S(1)} %copy-done, bf16[4096,512]{1,0:T(8,128)(2,1)} %bitcast.32, bf16[4096,512]{1,0:T(8,128)(2,1)} %bitcast.31, bf16[4096,512]{1,0:T(8,128)(2,1)} %param.24, ...), kind=kOutput, calls=%fused_computation.31 | convolution fusion | flops 8644456448 | bytes 23089152 | tf_op jit(solution)/shard_map/dot_general | solution.py:20
  129.9 4.9 %multiply_reduce_fusion = f32[4096]{0:T(1024)S(1)} fusion(f32[4096,512]{0,1:T(8,128)} %get-tuple-element.229, f32[4096]{0:T(1024)S(1)} %broadcast_multiply_fusion, f32[512]{0:T(512)S(1)} %copy-done.6), kind=kLoop, calls=%fused_computation.29 | loop fusion | flops 8384512 | bytes 8423424 | tf_op jit(solution)/shard_map/reduce_sum | solution.py:22
  134.8 0.8 copy-done.1
  135.7 6.5 %select_convert_fusion = bf16[4096,512]{0,1:T(8,128)(2,1)} fusion(bf16[4096,512]{0,1:T(8,128)(2,1)} %copy.19, f32[4096,512]{0,1:T(8,128)S(1)} %copy-done.1, f32[512]{0:T(512)S(1)} %copy-done.7, f32[512]{0:T(512)S(1)} %copy-done.8, f32[4096]{0:T(1024)S(1)} %add_rsqrt_fusion, f32[4096]{0:T(1024)S(1)} %broadcast_multiply_fusion, f32[512]{0:T(512)S(1)} %copy-done.6, ...), kind=kLoop, calls=%fused_computation.28 | loop fusion | flops 18874368 | bytes 16820224 | tf_op jit(solution)/shard_map/convert_element_type | solution.py:82
  142.2 6.4 %copy.22 = bf16[4096,512]{1,0:T(8,128)(2,1)} copy(bf16[4096,512]{0,1:T(8,128)(2,1)} %select_convert_fusion) | data formatting | bytes 8388608
  148.6 13.3 %while.38 = (s32[]{:T(128)}, f32[512,512]{1,0:T(8,128)S(1)}, s32[4096]{0:T(1024)S(1)}, bf16[4096,512]{1,0:T(8,128)(2,1)}, s32[]{:T(128)}, /*index=5*/s32[]{:T(128)}, s32[]{:T(128)}, s32[]{:T(128)}) while((s32[]{:T(128)}, f32[512,512]{1,0:T(8,128)S(1)}, s32[4096]{0:T(1024)S(1)}, bf16[4096,512]{1,0:T(8,128)(2,1)}, s32[]{:T(128)}, ...), condition=%wide.region_7.8_spmd.clone, body=%wide.region_6.7_spmd.clone.sunk | while | flops 269221888 | bytes 2627733 | solution.py:94
  148.6 1.6 convolution_add_fusion.4
  150.2 0.1 dynamic_slice.36
  150.3 1.6 convolution_add_fusion.4
  151.9 0.1 dynamic_slice.36
  152.0 1.6 convolution_add_fusion.4
  153.6 1.6 convolution_add_fusion.4
  155.3 1.6 convolution_add_fusion.4
  157.0 1.6 convolution_add_fusion.4
  158.7 1.6 convolution_add_fusion.4
  160.3 1.6 convolution_add_fusion.4
  161.9 0.9 convert_element_type.36
  162.8 2.8 %fusion.48 = (f32[512]{0:T(512)S(1)}, f32[512,512]{0,1:T(8,128)S(1)}) fusion(f32[512]{0:T(512)S(1)} %copy-done.12, bf16[512,512]{1,0:T(8,128)(2,1)} %param.36, bf16[1024,512]{1,0:T(8,128)(2,1)} %param.34, bf16[512,512]{1,0:T(8,128)(2,1)} %convert_element_type.36, bf16[512,512]{1,0:T(8,128)(2,1)S(1)} %get-tuple-element.361, f32[512]{0:T(512)S(1)} %copy-done.13), kind=kOutput, calls=%fused_computation.71 | convolution fusion | flops 809500160 | bytes 3676160 | tf_op jit(solution)/shard_map/dot_general | solution.py:20
  165.6 0.2 multiply_reduce_fusion.1
  165.8 1.3 add_convert_fusion
  167.2 1.0 copy.23
  (74 shorter events, 0.7 us)
Async XLA Ops:
  0.6 115.3 %copy-start = (bf16[1536,512]{1,0:T(8,128)(2,1)S(1)}, bf16[1536,512]{1,0:T(8,128)(2,1)}, u32[]{:S(2)}) copy-start(bf16[1536,512]{1,0:T(8,128)(2,1)} %param.28) | copy-start | bytes 4718596
  0.6 16.8 %slice-start = ((bf16[512,512]{1,0:T(8,128)(2,1)}), bf16[16,512]{1,0:T(8,128)(2,1)S(1)}, s32[]{:S(2)}) async-start(bf16[512,512]{1,0:T(8,128)(2,1)} %param.23), calls=%async_computation | async-start | bytes 32768 | tf_op jit(solution)/shard_map/slice | solution.py:64
  0.7 16.1 %copy-start.3 = (s32[4096]{0:T(1024)S(1)}, s32[4096]{0:T(1024)}, u32[]{:S(2)}) copy-start(s32[4096]{0:T(1024)} %param.26) | copy-start | bytes 49156
  2.3 57.5 %copy-start.2 = (bf16[512,512]{1,0:T(8,128)(2,1)S(1)}, bf16[512,512]{1,0:T(8,128)(2,1)}, u32[]{:S(2)}) copy-start(bf16[512,512]{1,0:T(8,128)(2,1)} %param.23) | copy-start | bytes 1572868
  4.9 73.7 %collective-permute-start = (bf16[32,512]{1,0:T(8,128)(2,1)S(1)}, bf16[32,512]{1,0:T(8,128)(2,1)}, u32[]{:S(2)}, u32[]{:S(2)}) collective-permute-start(bf16[32,512]{1,0:T(8,128)(2,1)S(1)} %get-tuple-element.227), channel_id=1, source_target_pairs={{31,0},{0,1},{1,2},{2,3},{3,4},{4,5},{5,6},{6,7},{7,8},{8,9},{9,10... | collective-permute-start | bytes 98312 | tf_op jit(solution)/shard_map/ppermute | solution.py:15
  5.4 74.5 %collective-permute-start.1 = (bf16[32,512]{1,0:T(8,128)(2,1)S(1)}, bf16[32,512]{1,0:T(8,128)(2,1)}, u32[]{:S(2)}, u32[]{:S(2)}) collective-permute-start(bf16[32,512]{1,0:T(8,128)(2,1)S(1)} %get-tuple-element.226), channel_id=1, source_target_pairs={{1,0},{2,1},{3,2},{4,3},{5,4},{6,5},{7,6},{8,7},{9,8},{10,9},{11,1... | collective-permute-start | bytes 98312 | tf_op jit(solution)/shard_map/ppermute | solution.py:15
  11.4 71.6 %collective-permute-start.2 = (bf16[32,512]{1,0:T(8,128)(2,1)S(1)}, bf16[32,512]{1,0:T(8,128)(2,1)S(1)}, u32[]{:S(2)}, u32[]{:S(2)}) collective-permute-start(bf16[32,512]{1,0:T(8,128)(2,1)S(1)} %get-tuple-element.225), channel_id=1, source_target_pairs={{25,0},{26,1},{27,2},{28,3},{29,4},{30,5},{31,6},{0,7},{1,8},{2,9}... | collective-permute-start | bytes 98312 | tf_op jit(solution)/shard_map/ppermute | solution.py:15
  11.4 75.0 %collective-permute-start.3 = (bf16[32,512]{1,0:T(8,128)(2,1)S(1)}, bf16[32,512]{1,0:T(8,128)(2,1)S(1)}, u32[]{:S(2)}, u32[]{:S(2)}) collective-permute-start(bf16[32,512]{1,0:T(8,128)(2,1)S(1)} %get-tuple-element.224), channel_id=1, source_target_pairs={{7,0},{8,1},{9,2},{10,3},{11,4},{12,5},{13,6},{14,7},{15,8},{16,9}... | collective-permute-start | bytes 98312 | tf_op jit(solution)/shard_map/ppermute | solution.py:15
  14.9 72.0 %collective-permute-start.4 = (bf16[32,512]{1,0:T(8,128)(2,1)S(1)}, bf16[32,512]{1,0:T(8,128)(2,1)S(1)}, u32[]{:S(2)}, u32[]{:S(2)}) collective-permute-start(bf16[32,512]{1,0:T(8,128)(2,1)S(1)} %get-tuple-element.223), channel_id=1, source_target_pairs={{24,0},{25,1},{26,2},{27,3},{28,4},{29,5},{30,6},{31,7},{0,8},{1,9... | collective-permute-start | bytes 98312 | tf_op jit(solution)/shard_map/ppermute | solution.py:15
  59.9 12.4 %copy-start.4 = (s32[4096]{0:T(1024)S(1)}, s32[4096]{0:T(1024)}, u32[]{:S(2)}) copy-start(s32[4096]{0:T(1024)} %param.25) | copy-start | bytes 49156
  78.5 9.1 %collective-permute-start.5 = (bf16[32,512]{1,0:T(8,128)(2,1)S(1)}, bf16[32,512]{1,0:T(8,128)(2,1)S(1)}, u32[]{:S(2)}, u32[]{:S(2)}) collective-permute-start(bf16[32,512]{1,0:T(8,128)(2,1)S(1)} %get-tuple-element.222), channel_id=1, source_target_pairs={{8,0},{9,1},{10,2},{11,3},{12,4},{13,5},{14,6},{15,7},{16,8},{17,9... | collective-permute-start | bytes 98312 | tf_op jit(solution)/shard_map/ppermute | solution.py:15
  79.9 8.3 %collective-permute-start.6 = (bf16[32,512]{1,0:T(8,128)(2,1)S(1)}, bf16[32,512]{1,0:T(8,128)(2,1)S(1)}, u32[]{:S(2)}, u32[]{:S(2)}) collective-permute-start(bf16[32,512]{1,0:T(8,128)(2,1)S(1)} %get-tuple-element.221), channel_id=1, source_target_pairs={{23,0},{24,1},{25,2},{26,3},{27,4},{28,5},{29,6},{30,7},{31,8},{0,... | collective-permute-start | bytes 98312 | tf_op jit(solution)/shard_map/ppermute | solution.py:15
  83.0 5.8 %collective-permute-start.7 = (bf16[32,512]{1,0:T(8,128)(2,1)S(1)}, bf16[32,512]{1,0:T(8,128)(2,1)S(1)}, u32[]{:S(2)}, u32[]{:S(2)}) collective-permute-start(bf16[32,512]{1,0:T(8,128)(2,1)S(1)} %get-tuple-element.220), channel_id=1, source_target_pairs={{9,0},{10,1},{11,2},{12,3},{13,4},{14,5},{15,6},{16,7},{17,8},{18,... | collective-permute-start | bytes 98312 | tf_op jit(solution)/shard_map/ppermute | solution.py:15
  91.8 24.2 %copy-start.6 = (f32[512]{0:T(512)S(1)}, f32[512]{0:T(512)}, u32[]{:S(2)}) copy-start(f32[512]{0:T(512)} %param.31) | copy-start | bytes 6148
  91.8 24.2 %copy-start.11 = (f32[512]{0:T(512)S(1)}, f32[512]{0:T(512)}, u32[]{:S(2)}) copy-start(f32[512]{0:T(512)} %param.29) | copy-start | bytes 6148
  129.9 5.8 %copy-start.1 = (f32[4096,512]{0,1:T(8,128)S(1)}, f32[4096,512]{0,1:T(8,128)}, u32[]{:S(2)}) copy-start(f32[4096,512]{0,1:T(8,128)} %get-tuple-element.229) | copy-start | bytes 25165828
  129.9 5.8 %copy-start.5 = (pred[4096]{0:T(1024)(128)(4,1)S(1)}, pred[4096]{0:T(1024)(128)(4,1)}, u32[]{:S(2)}) copy-start(pred[4096]{0:T(1024)(128)(4,1)} %broadcast_compare_fusion) | copy-start | bytes 12292
  129.9 5.8 %copy-start.7 = (f32[512]{0:T(512)S(1)}, f32[512]{0:T(512)}, u32[]{:S(2)}) copy-start(f32[512]{0:T(512)} %param.33) | copy-start | bytes 6148
  129.9 5.7 %copy-start.8 = (f32[512]{0:T(512)S(1)}, f32[512]{0:T(512)}, u32[]{:S(2)}) copy-start(f32[512]{0:T(512)} %param.32) | copy-start | bytes 6148
  148.6 14.2 %copy-start.12 = (f32[512]{0:T(512)S(1)}, f32[512]{0:T(512)}, u32[]{:S(2)}) copy-start(f32[512]{0:T(512)} %param.37) | copy-start | bytes 6148
  148.6 14.2 %copy-start.13 = (f32[512]{0:T(512)S(1)}, f32[512]{0:T(512)}, u32[]{:S(2)}) copy-start(f32[512]{0:T(512)} %param.35) | copy-start | bytes 6148
  162.8 3.0 %copy-start.9 = (f32[512]{0:T(512)S(1)}, f32[512]{0:T(512)}, u32[]{:S(2)}) copy-start(f32[512]{0:T(512)} %param.39) | copy-start | bytes 6148
  162.8 3.0 %copy-start.10 = (f32[512]{0:T(512)S(1)}, f32[512]{0:T(512)}, u32[]{:S(2)}) copy-start(f32[512]{0:T(512)} %param.38) | copy-start | bytes 6148
where the time goes:
time: 169 us; the launch traced here: 168 us
  matrix products  63.8 us (38%)
  blocking collectives  40.1 us (24%)
  local copies, waits for them, and re-layouts  34.2 us (20%)
  other arithmetic  14.5 us (9%)
  starting transfers between devices  14.5 us (9%)
    all_gather x1, blocking collectives, on_device(): coarse_all = lax.all_gather(coarse, 'region', axis=0, tiled=True)  40.1 us
    dot_general x16, matrix products, select(): jnp.dot(one_hot, source, preferred_element_type=jnp.float32)  34.6 us
    unnamed x41, local copies, waits for them, and re-layouts  24.2 us
    dot_general x2, matrix products, finish(): jnp.dot(hidden, w_second, preferred_element_type=jnp.float32) + b_second  16.7 us
    ppermute x8, starting transfers between devices, from_behind(): return lax.ppermute(block, axis, route)  14.5 us
    dot_general x8, matrix products, add_block(): jnp.dot(one_hot, block_rows, preferred_element_type=jnp.float32)  12.5 us
    convert_element_type x1, other arithmetic, on_device(): jnp.where(live[:, None], edge_feat.astype(jnp.float32) + update, 0.0)  6.5 us
    reduce_sum x2, other arithmetic, finish(): var = jnp.mean((out - mean) ** 2, axis=-1, keepdims=True)  5.05 us
  transfers between devices with their start and end apart: 8, of which 0 were waited for; matrix products, arithmetic and copies ran while one was open for 17% of the time, Pallas kernels for 0%

commit v1 on v0

v1 whole, which is shorter than its diff:
```python
import functools

import jax
import jax.numpy as jnp
from jax import lax
from jax.experimental import pallas as pl
from jax.experimental.pallas import tpu as pltpu
from jax.sharding import PartitionSpec as P

COARSE_DEV = 16
NEIGHBOUR_STEPS = (1, -1, 7, -7, 8, -8, 9, -9)
MESH = pl.DeviceIdType.MESH
LANES = 128
F32 = jnp.float32
BF16 = jnp.bfloat16


def digits_of(n):
    bits = (n // 2).bit_length() - 1
    second = 1 << (bits // 2)
    return n // 2 // second, second, 2


def one_hot_rows(index_ref, first_group, groups, start, count):
    lane = lax.broadcasted_iota(jnp.int32, (LANES, LANES), 1)
    parts = []
    for g in range(groups):
        row = index_ref[pl.ds(first_group + g, 1), :]
        spread = jnp.broadcast_to(row, (LANES, LANES)).T - start
        parts.append(
            jnp.concatenate(
                [
                    jnp.where(spread == lane + c, 1.0, 0.0).astype(BF16)
                    for c in range(0, count, LANES)
                ],
                axis=1,
            )
        )
    return jnp.concatenate(parts, axis=0)


def one_hot_columns(index_ref, first_group, groups, count):
    parts = []
    for g in range(groups):
        row = index_ref[pl.ds(first_group + g, 1), :]
        ids = lax.broadcasted_iota(jnp.int32, (count, LANES), 0)
        parts.append(jnp.where(ids == row, 1.0, 0.0).astype(BF16))
    return jnp.concatenate(parts, axis=1)


def silu(x):
    half = 0.5 * x
    return half + half * jnp.tanh(half)


def layer_norm(y, gain, shift):
    inv = 1.0 / y.shape[1]
    y = y - jnp.sum(y, axis=1, keepdims=True) * inv
    var = jnp.sum(y * y, axis=1, keepdims=True) * inv
    return y * lax.rsqrt(var + 1e-5) * gain + shift


def exchange_kernel(
    n,
    block,
    node_hbm,
    edge_hbm,
    snd_ref,
    rcv_ref,
    sl_ref,
    w1_hbm,
    b1_ref,
    pre_hbm,
    coarse_out,
    halo_out,
    node_v,
    wsr_v,
    edge_v,
    pre_v,
    wcat,
    picked,
    load_sem,
    edge_sem,
    pre_sem,
    own_sem,
    send0,
    recv0,
    send1,
    recv1,
    send2,
    recv2,
    sendh,
    recvh,
):
    me = lax.axis_index("region")
    r0, r1, r2 = digits_of(n)
    d0, d1, d2 = me // (r1 * r2), (me // r2) % r1, me % r2
    nodes, width = node_v.shape
    blocks = edge_v.shape[0] // block
    groups = block // LANES
    neighbours, slots = sl_ref.shape

    def device(a, b, c):
        return ((a * r1 + b) * r2 + c,)

    def flip(d, k, r):
        out = jnp.int32(0)
        bit = 1
        while bit < r:
            have = (d // bit) % 2
            out = out + bit * (1 - have if k & bit else have)
            bit *= 2
        return out

    peers0 = [device(flip(d0, k, r0), d1, d2) for k in range(1, r0)]
    peers1 = [device(d0, flip(d1, k, r1), d2) for k in range(1, r1)]
    twin = device(d0, d1, 1 - d2)
    targets = [((me + step + n) % n,) for step in NEIGHBOUR_STEPS]

    load_node = pltpu.make_async_copy(node_hbm, node_v, load_sem.at[0])
    load_s = pltpu.make_async_copy(
        w1_hbm.at[pl.ds(width, width)], wsr_v.at[pl.ds(0, width)], load_sem.at[1]
    )
    load_r = pltpu.make_async_copy(
        w1_hbm.at[pl.ds(2 * width, width)], wsr_v.at[pl.ds(width, width)], load_sem.at[2]
    )
    load_e = pltpu.make_async_copy(
        w1_hbm.at[pl.ds(0, width)], wcat.at[pl.ds(0, width)], load_sem.at[3]
    )
    load_node.start()
    load_s.start()
    load_r.start()
    load_e.start()

    def edge_copy(i):
        rows = pl.ds(pl.multiple_of(i * block, block), block)
        return pltpu.make_async_copy(edge_hbm.at[rows], edge_v.at[rows], edge_sem.at[i])

    def pre_copy(i):
        rows = pl.ds(pl.multiple_of(i * block, block), block)
        return pltpu.make_async_copy(pre_v.at[rows], pre_hbm.at[rows], pre_sem.at[i])

    for i in range(blocks):
        edge_copy(i).start()

    barrier = pltpu.get_barrier_semaphore()
    greeted = peers0 + peers1 + [twin] + targets
    for target in greeted:
        pl.semaphore_signal(barrier, inc=1, device_id=target, device_id_type=MESH)

    load_node.wait()
    load_s.wait()
    sent_at = nodes + width
    wcat[pl.ds(sent_at, nodes), :] = jnp.dot(
        node_v[...], wsr_v[pl.ds(0, width), :], preferred_element_type=F32
    ).astype(BF16)

    mine = wcat.at[pl.ds(sent_at, COARSE_DEV)]
    own = pltpu.make_async_copy(mine, coarse_out.at[d0, d1, d2], own_sem)
    own.start()
    pl.semaphore_wait(barrier, len(greeted))
    stage0 = [
        pltpu.make_async_remote_copy(
            src_ref=mine,
            dst_ref=coarse_out.at[d0, d1, d2],
            send_sem=send0.at[k],
            recv_sem=recv0.at[k],
            device_id=peer,
            device_id_type=MESH,
        )
        for k, peer in enumerate(peers0)
    ]
    for copy in stage0:
        copy.start()

    ids = lax.broadcasted_iota(jnp.int32, (nodes, slots), 0)
    halo = []
    for j, target in enumerate(targets):
        wanted = jnp.where(ids == sl_ref[j : j + 1, :], 1.0, 0.0).astype(BF16)
        picked[j] = lax.dot_general(
            wanted,
            wcat[pl.ds(sent_at, nodes), :],
            (((0,), (0,)), ((), ())),
            preferred_element_type=F32,
        ).astype(BF16)
        copy = pltpu.make_async_remote_copy(
            src_ref=picked.at[j],
            dst_ref=halo_out.at[j],
            send_sem=sendh.at[j],
            recv_sem=recvh.at[j],
            device_id=target,
            device_id_type=MESH,
        )
        copy.start()
        halo.append(copy)

    load_r.wait()
    load_e.wait()
    wcat[pl.ds(width, nodes), :] = jnp.dot(
        node_v[...], wsr_v[pl.ds(width, width), :], preferred_element_type=F32
    ).astype(BF16)

    def one_block(i, carry):
        edge_copy(i).wait()
        rows = pl.ds(pl.multiple_of(i * block, block), block)
        left = jnp.concatenate(
            [
                edge_v[rows, :],
                one_hot_rows(rcv_ref, i * groups, groups, 0, nodes),
                one_hot_rows(snd_ref, i * groups, groups, 0, nodes),
            ],
            axis=1,
        )
        pre_v[rows, :] = jnp.dot(left, wcat[...], preferred_element_type=F32) + b1_ref[...]
        pre_copy(i).start()
        return carry

    cut1, cut2 = blocks // 4, 5 * blocks // 8
    lax.fori_loop(0, cut1, one_block, 0)

    own.wait()
    for copy in stage0:
        copy.wait_recv()

    def column_to(peer, digit, send_sem, recv_sem):
        column = coarse_out.at[:, digit, d2]
        return pltpu.make_async_remote_copy(
            src_ref=column,
            dst_ref=column,
            send_sem=send_sem,
            recv_sem=recv_sem,
            device_id=peer,
            device_id_type=MESH,
        )

    stage1 = [
        column_to(peer, d1, send1.at[k], recv1.at[k]) for k, peer in enumerate(peers1)
    ]
    stage2 = [
        column_to(twin, flip(d1, m, r1), send2.at[m], recv2.at[m]) for m in range(r1)
    ]
    for copy in stage1:
        copy.start()
    stage2[0].start()

    lax.fori_loop(cut1, cut2, one_block, 0)
    for k, copy in enumerate(stage1):
        copy.wait_recv()
        stage2[k + 1].start()
    lax.fori_loop(cut2, blocks, one_block, 0)

    for i in range(blocks):
        pre_copy(i).wait()
    for copy in halo:
        copy.wait()
    for copy in stage2:
        copy.wait()
    for copy in stage0 + stage1:
        copy.wait_send()


def update_kernel(
    block,
    pre_hbm,
    edge_hbm,
    coarse_hbm,
    halo_hbm,
    node_hbm,
    snd_ref,
    rcv_ref,
    w2_hbm,
    b2_ref,
    gain_ref,
    shift_ref,
    nw1_hbm,
    nb1_ref,
    nw2_hbm,
    nb2_ref,
    ngain_ref,
    nshift_ref,
    edge_out,
    node_out,
    pre_v,
    edge_v,
    out_v,
    table,
    node_v,
    w2_v,
    nw1_v,
    nw2_v,
    total,
    load_sem,
    pre_sem,
    edge_sem,
    out_sem,
):
    nodes, width = node_v.shape
    blocks = edge_v.shape[0] // block
    groups = block // LANES
    coarse_rows = coarse_hbm.shape[0]
    halo_rows = halo_hbm.shape[0]

    def rows_of(i):
        return pl.ds(pl.multiple_of(i * block, block), block)

    def pre_copy(i):
        rows = rows_of(i)
        return pltpu.make_async_copy(pre_hbm.at[rows], pre_v.at[rows], pre_sem.at[i])

    def edge_copy(i):
        rows = rows_of(i)
        return pltpu.make_async_copy(edge_hbm.at[rows], edge_v.at[rows], edge_sem.at[i])

    def out_copy(i):
        rows = rows_of(i)
        return pltpu.make_async_copy(out_v.at[rows], edge_out.at[rows], out_sem.at[i])

    loads = [
        pltpu.make_async_copy(source, place, load_sem.at[k])
        for k, (source, place) in enumerate(
            [
                (coarse_hbm, table.at[pl.ds(0, coarse_rows)]),
                (halo_hbm, table.at[pl.ds(coarse_rows, halo_rows)]),
                (w2_hbm, w2_v),
                (node_hbm, node_v),
                (nw1_hbm, nw1_v),
                (nw2_hbm, nw2_v),
            ]
        )
    ]
    for load in loads[:2]:
        load.start()
    pre_copy(0).start()
    loads[2].start()
    edge_copy(0).start()
    for i in range(1, blocks):
        pre_copy(i).start()
        edge_copy(i).start()
    for load in loads[3:]:
        load.start()
    total[...] = jnp.zeros_like(total)
    for load in loads[:3]:
        load.wait()

    def one_block(i, carry):
        pre_copy(i).wait()
        edge_copy(i).wait()
        rows = rows_of(i)
        wanted = one_hot_rows(snd_ref, i * groups, groups, nodes, coarse_rows + halo_rows)
        pre = pre_v[rows, :] + jnp.dot(wanted, table[...], preferred_element_type=F32)
        hidden = silu(pre).astype(BF16)
        y = jnp.dot(hidden, w2_v[...], preferred_element_type=F32) + b2_ref[...]
        new = edge_v[rows, :].astype(F32) + layer_norm(y, gain_ref[...], shift_ref[...])
        live = []
        for g in range(groups):
            row = rcv_ref[pl.ds(i * groups + g, 1), :]
            live.append(jnp.broadcast_to(row, (LANES, LANES)).T[:, :1])
        live = jnp.concatenate(live, axis=0) < nodes
        new = jnp.where(live, new, 0.0).astype(BF16)
        out_v[rows, :] = new
        out_copy(i).start()
        total[...] += jnp.dot(
            one_hot_columns(rcv_ref, i * groups, groups, nodes),
            new,
            preferred_element_type=F32,
        )
        return carry

    lax.fori_loop(0, blocks, one_block, 0)

    for load in loads[3:]:
        load.wait()
    node = node_v[...]
    both = jnp.concatenate([node, total[...].astype(BF16)], axis=1)
    pre = jnp.dot(both, nw1_v[...], preferred_element_type=F32) + nb1_ref[...]
    y = jnp.dot(silu(pre).astype(BF16), nw2_v[...], preferred_element_type=F32) + nb2_ref[...]
    node_out[...] = (
        node.astype(F32) + layer_norm(y, ngain_ref[...], nshift_ref[...])
    ).astype(BF16)
    for i in range(blocks):
        out_copy(i).wait()


def on_device(
    node_feat,
    edge_feat,
    sender,
    receiver,
    send_list,
    edge_w1,
    edge_b1,
    edge_w2,
    edge_b2,
    edge_gain,
    edge_shift,
    node_w1,
    node_b1,
    node_w2,
    node_b2,
    node_gain,
    node_shift,
):
    n = lax.axis_size("region")
    nodes, width = node_feat.shape
    edges = edge_feat.shape[0]
    neighbours, slots = send_list.shape[1:]
    block = min(512, edges)
    blocks = edges // block
    digits = digits_of(n)
    vmem = pl.BlockSpec(memory_space=pltpu.VMEM)
    hbm = pl.BlockSpec(memory_space=pl.ANY)
    dma = pltpu.SemaphoreType.DMA
    snd = sender.reshape(edges // LANES, LANES)
    rcv = receiver.reshape(edges // LANES, LANES)

    def row(vector):
        return vector.reshape(1, width)

    pre, coarse, halo = pl.pallas_call(
        functools.partial(exchange_kernel, n, block),
        out_shape=(
            jax.ShapeDtypeStruct((edges, width), F32),
            jax.ShapeDtypeStruct(digits + (COARSE_DEV, width), BF16),
            jax.ShapeDtypeStruct((neighbours, slots, width), BF16),
        ),
        in_specs=[hbm, hbm, vmem, vmem, vmem, hbm, vmem],
        out_specs=(hbm, hbm, hbm),
        scratch_shapes=[
            pltpu.VMEM((nodes, width), BF16),
            pltpu.VMEM((2 * width, width), BF16),
            pltpu.VMEM((edges, width), BF16),
            pltpu.VMEM((edges, width), F32),
            pltpu.VMEM((width + 2 * nodes, width), BF16),
            pltpu.VMEM((neighbours, slots, width), BF16),
            dma((4,)),
            dma((blocks,)),
            dma((blocks,)),
            dma,
            dma((digits[0] - 1,)),
            dma((digits[0] - 1,)),
            dma((digits[1] - 1,)),
            dma((digits[1] - 1,)),
            dma((digits[1],)),
            dma((digits[1],)),
            dma((neighbours,)),
            dma((neighbours,)),
        ],
        compiler_params=pltpu.CompilerParams(
            collective_id=0, has_side_effects=True, vmem_limit_bytes=48 * 2**20
        ),
        cost_estimate=pl.CostEstimate(
            flops=2 * edges * (width + 2 * nodes) * width,
            bytes_accessed=6 * edges * width,
            transcendentals=0,
        ),
        name="exchange",
    )(node_feat, edge_feat, snd, rcv, send_list[0], edge_w1, row(edge_b1))

    coarse_rows = n * COARSE_DEV
    halo_rows = neighbours * slots
    return pl.pallas_call(
        functools.partial(update_kernel, block),
        out_shape=(
            jax.ShapeDtypeStruct((edges, width), BF16),
            jax.ShapeDtypeStruct((nodes, width), BF16),
        ),
        in_specs=[hbm] * 5 + [vmem] * 2 + [hbm] + [vmem] * 3 + [hbm, vmem, hbm] + [vmem] * 3,
        out_specs=(hbm, vmem),
        scratch_shapes=[
            pltpu.VMEM((edges, width), F32),
            pltpu.VMEM((edges, width), BF16),
            pltpu.VMEM((edges, width), BF16),
            pltpu.VMEM((coarse_rows + halo_rows, width), BF16),
            pltpu.VMEM((nodes, width), BF16),
            pltpu.VMEM(edge_w2.shape, BF16),
            pltpu.VMEM(node_w1.shape, BF16),
            pltpu.VMEM(node_w2.shape, BF16),
            pltpu.VMEM((nodes, width), F32),
            dma((6,)),
            dma((blocks,)),
            dma((blocks,)),
            dma((blocks,)),
        ],
        compiler_params=pltpu.CompilerParams(vmem_limit_bytes=48 * 2**20),
        cost_estimate=pl.CostEstimate(
            flops=2 * edges * (2 * width + coarse_rows + halo_rows) * width,
            bytes_accessed=8 * edges * width,
            transcendentals=edges * width,
        ),
        name="update",
    )(
        pre,
        edge_feat,
        coarse.reshape(coarse_rows, width),
        halo.reshape(halo_rows, width),
        node_feat,
        snd,
        rcv,
        edge_w2,
        row(edge_b2),
        row(edge_gain),
        row(edge_shift),
        node_w1,
        row(node_b1),
        node_w2,
        row(node_b2),
        row(node_gain),
        row(node_shift),
    )


def solution(mesh):
    split2, split1, whole = P("region", None), P("region"), P()
    in_specs = (split2, split2, split1, split1, P("region", None, None)) + (whole,) * 12
    return jax.shard_map(
        on_device, mesh=mesh, in_specs=in_specs, out_specs=(split2, split2), check_vma=False
    )
```

time: 169 us -> 45.6 us (0.27)
  matrix products: 63.8 us -> 0 us
  blocking collectives: 40.1 us -> 0 us
  Pallas kernels: 0 us -> 39.1 us
  local copies, waits for them, and re-layouts: 34.2 us -> 5.28 us
  other arithmetic: 14.5 us -> 0 us
  starting transfers between devices: 14.5 us -> 0 us
    dot_general x26 -> x0, matrix products: 63.8 us -> none  [the longest x16 34.6 us: select(): jnp.dot(one_hot, source, preferred_element_type=jnp.float32)]
    all_gather x1 -> x0, blocking collectives: 40.1 us -> none  [on_device(): coarse_all = lax.all_gather(coarse, 'region', axis=0, tiled=True)]
    pallas_call x0 -> x2, Pallas kernels: none -> 39.1 us  [the longest x1 20.9 us: on_device(): pl.pallas_call(functools.partial(exchange_kernel, n, block), out_shape=(j...]
    unnamed x41 -> x32, local copies, waits for them, and re-layouts: 24.2 us -> 5.28 us
    ppermute x8 -> x0, starting transfers between devices: 14.5 us -> none  [from_behind(): return lax.ppermute(block, axis, route)]
    convert_element_type x3 -> x0, other arithmetic: 8.7 us -> none  [the longest x1 6.5 us: on_device(): jnp.where(live[:, None], edge_feat.astype(jnp.float32) + update, 0.0)]
    another operation x5 -> x0, local copies, waits for them, and re-layouts: 6.28 us -> none
    reduce_sum x2 -> x0, other arithmetic: 5.05 us -> none  [finish(): var = jnp.mean((out - mean) ** 2, axis=-1, keepdims=True)]
  transfers between devices with their start and end apart: 8 -> 0, of which waited for: 0 -> 0; matrix products, arithmetic and copies ran while one was open for 17% -> 0% of each run, Pallas kernels for 0% -> 0%
where the time goes in v1:
time: 45.6 us; the launch traced here: 45.2 us
  Pallas kernels  39.1 us (86%)
  local copies, waits for them, and re-layouts  5.28 us (12%)
  between operations  0.79 us (2%)
    pallas_call x1, Pallas kernels, on_device(): pl.pallas_call(functools.partial(exchange_kernel, n, block), out_shape=(j...  20.9 us
    pallas_call x1, Pallas kernels, on_device(): pl.pallas_call(functools.partial(update_kernel, block), out_shape=(jax.Sh...  18.2 us
    unnamed x32, local copies, waits for them, and re-layouts  5.28 us

profile of v1, /device:TPU:0, one launch (start us, length us, event | category | flops | bytes accessed | tf_op | source)
XLA Modules:
  0.0 45.2 jit_solution(11099229151669059595)
XLA Ops:
  0.6 0.0 copy-start
  0.6 1.4 %copy-done = bf16[1536,512]{1,0:T(8,128)(2,1)S(1)} copy-done((bf16[1536,512]{1,0:T(8,128)(2,1)S(1)}, bf16[1536,512]{1,0:T(8,128)(2,1)}, u32[]{:S(2)}) %copy-start) | copy-done | bytes 1572888
  2.0 0.0 copy-start.2
  2.0 1.0 %copy-done.2 = bf16[512,512]{1,0:T(8,128)(2,1)S(1)} copy-done((bf16[512,512]{1,0:T(8,128)(2,1)S(1)}, bf16[512,512]{1,0:T(8,128)(2,1)}, u32[]{:S(2)}) %copy-start.2) | copy-done | bytes 524312
  3.1 0.0 copy-start.5
  3.1 0.7 %copy-done.5 = s32[4096]{0:T(1024)S(1)} copy-done((s32[4096]{0:T(1024)S(1)}, s32[4096]{0:T(1024)}, u32[]{:S(2)}) %copy-start.5) | copy-done | bytes 16408
  3.8 0.0 copy-start.6
  3.8 0.7 %copy-done.6 = s32[4096]{0:T(1024)S(1)} copy-done((s32[4096]{0:T(1024)S(1)}, s32[4096]{0:T(1024)}, u32[]{:S(2)}) %copy-start.6) | copy-done | bytes 16408
  4.5 0.0 copy-start.7
  4.5 0.7 %copy-done.7 = s32[1,8,32]{2,1,0:T(8,128)S(1)} copy-done((s32[1,8,32]{2,1,0:T(8,128)S(1)}, s32[1,8,32]{2,1,0:T(8,128)}, u32[]{:S(2)}) %copy-start.7) | copy-done | bytes 1048
  5.2 0.0 copy-start.8
  5.2 0.7 %copy-done.8 = f32[512]{0:T(512)S(1)} copy-done((f32[512]{0:T(512)S(1)}, f32[512]{0:T(512)}, u32[]{:S(2)}) %copy-start.8) | copy-done | bytes 2072
  5.9 0.0 copy-start.1
  5.9 0.0 copy-start.3
  5.9 0.0 copy-start.4
  5.9 0.0 copy-start.9
  5.9 0.0 copy-start.10
  5.9 0.0 copy-start.11
  5.9 0.0 copy-start.12
  5.9 0.0 copy-start.13
  5.9 0.0 copy-start.14
  6.0 0.0 copy-start.15
  6.0 20.9 %exchange.1 = (f32[4096,512]{1,0:T(8,128)}, bf16[4,4,2,16,512]{4,3,2,1,0:T(8,128)(2,1)S(1)}, bf16[8,32,512]{2,1,0:T(8,128)(2,1)S(1)}) custom-call(bf16[512,512]{1,0:T(8,128)(2,1)S(1)} %copy-done.2, bf16[4096,512]{1,0:T(8,128)(2,1)} %edge_hbm.3, s32[32,128]{1,0:T(8,128)S(1)} %bitcast.13, s32[32,128]{1,0:T(8,128)S(1)} %bitcast.15, s32[8,32]{1,0:T(8,128)S(1)} %bitcast.17, ...), custom_call_target="tpu_custom_call" | custom-call | flops 6442450944 | bytes 12582912 | tf_op jit(solution)/shard_map/exchange/pallas_call | solution.py:419
  26.9 0.0 copy-done.1
  26.9 0.0 copy-done.3
  26.9 0.0 copy-done.4
  26.9 0.0 copy-done.9
  26.9 0.0 copy-done.10
  26.9 0.0 copy-done.11
  27.0 0.0 copy-done.12
  27.0 0.0 copy-done.13
  27.0 0.0 copy-done.14
  27.0 0.0 copy-done.15
  27.0 18.2 %update.1 = (bf16[4096,512]{1,0:T(8,128)(2,1)}, bf16[512,512]{1,0:T(8,128)(2,1)}) custom-call(f32[4096,512]{1,0:T(8,128)} %get-tuple-element.5.pre_hbm, bf16[4096,512]{1,0:T(8,128)(2,1)} %edge_hbm.3, bf16[512,512]{1,0:T(8,128)(2,1)S(1)} %bitcast.26, bf16[256,512]{1,0:T(8,128)(2,1)S(1)} %bitcast.27, bf16[512,512]{1,0:T(8,128)(2,1)S(1)} %copy-done.2, ...), custom_call_target="tpu_custom_call" | custom-call | flops 7516192768 | bytes 16777216 | tf_op jit(solution)/shard_map/update/pallas_call | solution.py:461
Async XLA Ops:
  0.6 1.4 %copy-start = (bf16[1536,512]{1,0:T(8,128)(2,1)S(1)}, bf16[1536,512]{1,0:T(8,128)(2,1)}, u32[]{:S(2)}) copy-start(bf16[1536,512]{1,0:T(8,128)(2,1)} %w1_hbm.1) | copy-start | bytes 4718596
  2.0 1.0 %copy-start.2 = (bf16[512,512]{1,0:T(8,128)(2,1)S(1)}, bf16[512,512]{1,0:T(8,128)(2,1)}, u32[]{:S(2)}) copy-start(bf16[512,512]{1,0:T(8,128)(2,1)} %node_hbm.3) | copy-start | bytes 1572868
  3.1 0.7 %copy-start.5 = (s32[4096]{0:T(1024)S(1)}, s32[4096]{0:T(1024)}, u32[]{:S(2)}) copy-start(s32[4096]{0:T(1024)} %param.19) | copy-start | bytes 49156
  3.8 0.7 %copy-start.6 = (s32[4096]{0:T(1024)S(1)}, s32[4096]{0:T(1024)}, u32[]{:S(2)}) copy-start(s32[4096]{0:T(1024)} %param.20) | copy-start | bytes 49156
  4.5 0.7 %copy-start.7 = (s32[1,8,32]{2,1,0:T(8,128)S(1)}, s32[1,8,32]{2,1,0:T(8,128)}, u32[]{:S(2)}) copy-start(s32[1,8,32]{2,1,0:T(8,128)} %param.21) | copy-start | bytes 3076
  5.2 0.7 %copy-start.8 = (f32[512]{0:T(512)S(1)}, f32[512]{0:T(512)}, u32[]{:S(2)}) copy-start(f32[512]{0:T(512)} %param.23) | copy-start | bytes 6148
  5.9 21.0 %copy-start.1 = (bf16[1024,512]{1,0:T(8,128)(2,1)S(1)}, bf16[1024,512]{1,0:T(8,128)(2,1)}, u32[]{:S(2)}) copy-start(bf16[1024,512]{1,0:T(8,128)(2,1)} %nw1_hbm.1) | copy-start | bytes 3145732
  5.9 21.0 %copy-start.3 = (bf16[512,512]{1,0:T(8,128)(2,1)S(1)}, bf16[512,512]{1,0:T(8,128)(2,1)}, u32[]{:S(2)}) copy-start(bf16[512,512]{1,0:T(8,128)(2,1)} %w2_hbm.1) | copy-start | bytes 1572868
  5.9 21.0 %copy-start.4 = (bf16[512,512]{1,0:T(8,128)(2,1)S(1)}, bf16[512,512]{1,0:T(8,128)(2,1)}, u32[]{:S(2)}) copy-start(bf16[512,512]{1,0:T(8,128)(2,1)} %nw2_hbm.1) | copy-start | bytes 1572868
  5.9 21.0 %copy-start.9 = (f32[512]{0:T(512)S(1)}, f32[512]{0:T(512)}, u32[]{:S(2)}) copy-start(f32[512]{0:T(512)} %param.25) | copy-start | bytes 6148
  5.9 21.0 %copy-start.10 = (f32[512]{0:T(512)S(1)}, f32[512]{0:T(512)}, u32[]{:S(2)}) copy-start(f32[512]{0:T(512)} %param.26) | copy-start | bytes 6148
  5.9 21.0 %copy-start.11 = (f32[512]{0:T(512)S(1)}, f32[512]{0:T(512)}, u32[]{:S(2)}) copy-start(f32[512]{0:T(512)} %param.27) | copy-start | bytes 6148
  5.9 21.0 %copy-start.12 = (f32[512]{0:T(512)S(1)}, f32[512]{0:T(512)}, u32[]{:S(2)}) copy-start(f32[512]{0:T(512)} %param.29) | copy-start | bytes 6148
  5.9 21.0 %copy-start.13 = (f32[512]{0:T(512)S(1)}, f32[512]{0:T(512)}, u32[]{:S(2)}) copy-start(f32[512]{0:T(512)} %param.31) | copy-start | bytes 6148
  5.9 21.0 %copy-start.14 = (f32[512]{0:T(512)S(1)}, f32[512]{0:T(512)}, u32[]{:S(2)}) copy-start(f32[512]{0:T(512)} %param.32) | copy-start | bytes 6148
  6.0 21.0 %copy-start.15 = (f32[512]{0:T(512)S(1)}, f32[512]{0:T(512)}, u32[]{:S(2)}) copy-start(f32[512]{0:T(512)} %param.33) | copy-start | bytes 6148

commit v2 on v1

--- a/solution.py
+++ b/solution.py
@@ -11,6 +11,7 @@
 NEIGHBOUR_STEPS = (1, -1, 7, -7, 8, -8, 9, -9)
 MESH = pl.DeviceIdType.MESH
 LANES = 128
+VMEM_BYTES = 64 * 2**20
 F32 = jnp.float32
 BF16 = jnp.bfloat16
 
@@ -22,34 +23,36 @@
 
 
 def one_hot_rows(index_ref, first_group, groups, start, count):
-    lane = lax.broadcasted_iota(jnp.int32, (LANES, LANES), 1)
+    lane = lax.broadcasted_iota(jnp.int32, (LANES, LANES), 1).astype(jnp.int16)
+    one, zero = jnp.ones((), BF16), jnp.zeros((), BF16)
     parts = []
     for g in range(groups):
-        row = index_ref[pl.ds(first_group + g, 1), :]
-        spread = jnp.broadcast_to(row, (LANES, LANES)).T - start
+        row = index_ref[pl.ds(first_group + g, 1), :] - start
+        spread = jnp.broadcast_to(row, (LANES, LANES)).T.astype(jnp.int16) - lane
         parts.append(
             jnp.concatenate(
-                [
-                    jnp.where(spread == lane + c, 1.0, 0.0).astype(BF16)
-                    for c in range(0, count, LANES)
-                ],
-                axis=1,
+                [jnp.where(spread == c, one, zero) for c in range(0, count, LANES)], axis=1
             )
         )
     return jnp.concatenate(parts, axis=0)
 
 
-def one_hot_columns(index_ref, first_group, groups, count):
+def one_hot_columns(index_ref, first_group, groups, start, count):
+    lane = lax.broadcasted_iota(jnp.int32, (LANES, LANES), 0)
+    one, zero = jnp.ones((), BF16), jnp.zeros((), BF16)
     parts = []
     for g in range(groups):
-        row = index_ref[pl.ds(first_group + g, 1), :]
-        ids = lax.broadcasted_iota(jnp.int32, (count, LANES), 0)
-        parts.append(jnp.where(ids == row, 1.0, 0.0).astype(BF16))
+        row = index_ref[pl.ds(first_group + g, 1), :] - start
+        spread = (row - lane).astype(jnp.int16)
+        parts.append(
+            jnp.concatenate(
+                [jnp.where(spread == c, one, zero) for c in range(0, count, LANES)], axis=0
+            )
+        )
     return jnp.concatenate(parts, axis=1)
 
 
-def silu(x):
-    half = 0.5 * x
+def silu_of_half(half):
     return half + half * jnp.tanh(half)
 
 
@@ -65,14 +68,18 @@
     block,
     node_hbm,
     edge_hbm,
+    snd_hbm,
+    rcv_hbm,
+    sl_hbm,
+    w1_hbm,
+    b1_hbm,
+    pre_hbm,
+    coarse_out,
+    halo_out,
     snd_ref,
     rcv_ref,
     sl_ref,
-    w1_hbm,
     b1_ref,
-    pre_hbm,
-    coarse_out,
-    halo_out,
     node_v,
     wsr_v,
     edge_v,
@@ -127,10 +134,19 @@
     load_e = pltpu.make_async_copy(
         w1_hbm.at[pl.ds(0, width)], wcat.at[pl.ds(0, width)], load_sem.at[3]
     )
+    small = [
+        pltpu.make_async_copy(source, place, load_sem.at[4 + k])
+        for k, (source, place) in enumerate(
+            [(sl_hbm, sl_ref), (b1_hbm, b1_ref), (snd_hbm, snd_ref), (rcv_hbm, rcv_ref)]
+        )
+    ]
     load_node.start()
     load_s.start()
+    small[0].start()
     load_r.start()
     load_e.start()
+    for load in small[1:]:
+        load.start()
 
     def edge_copy(i):
         rows = pl.ds(pl.multiple_of(i * block, block), block)
@@ -151,8 +167,8 @@
     load_node.wait()
     load_s.wait()
     sent_at = nodes + width
-    wcat[pl.ds(sent_at, nodes), :] = jnp.dot(
-        node_v[...], wsr_v[pl.ds(0, width), :], preferred_element_type=F32
+    wcat[pl.ds(sent_at, nodes), :] = (
+        0.5 * jnp.dot(node_v[...], wsr_v[pl.ds(0, width), :], preferred_element_type=F32)
     ).astype(BF16)
 
     mine = wcat.at[pl.ds(sent_at, COARSE_DEV)]
@@ -173,6 +189,7 @@
     for copy in stage0:
         copy.start()
 
+    small[0].wait()
     ids = lax.broadcasted_iota(jnp.int32, (nodes, slots), 0)
     halo = []
     for j, target in enumerate(targets):
@@ -196,9 +213,13 @@
 
     load_r.wait()
     load_e.wait()
-    wcat[pl.ds(width, nodes), :] = jnp.dot(
-        node_v[...], wsr_v[pl.ds(width, width), :], preferred_element_type=F32
+    for load in small[1:]:
+        load.wait()
+    wcat[pl.ds(0, width), :] = wcat[pl.ds(0, width), :] * jnp.asarray(0.5, BF16)
+    wcat[pl.ds(width, nodes), :] = (
+        0.5 * jnp.dot(node_v[...], wsr_v[pl.ds(width, width), :], preferred_element_type=F32)
     ).astype(BF16)
+    bias = 0.5 * b1_ref[...]
 
     def one_block(i, carry):
         edge_copy(i).wait()
@@ -211,7 +232,7 @@
             ],
             axis=1,
         )
-        pre_v[rows, :] = jnp.dot(left, wcat[...], preferred_element_type=F32) + b1_ref[...]
+        pre_v[rows, :] = jnp.dot(left, wcat[...], preferred_element_type=F32) + bias
         pre_copy(i).start()
         return carry
 
@@ -266,29 +287,35 @@
     coarse_hbm,
     halo_hbm,
     node_hbm,
-    snd_ref,
-    rcv_ref,
+    snd_hbm,
+    rcv_hbm,
     w2_hbm,
-    b2_ref,
-    gain_ref,
-    shift_ref,
+    b2_hbm,
+    gain_hbm,
+    shift_hbm,
     nw1_hbm,
-    nb1_ref,
+    nb1_hbm,
     nw2_hbm,
-    nb2_ref,
-    ngain_ref,
-    nshift_ref,
+    nb2_hbm,
+    ngain_hbm,
+    nshift_hbm,
     edge_out,
     node_out,
     pre_v,
     edge_v,
     out_v,
     table,
+    snd_ref,
+    rcv_ref,
+    w2_v,
+    rows_v,
     node_v,
-    w2_v,
     nw1_v,
     nw2_v,
     total,
+    hidden_a,
+    hidden_b,
+    new_node,
     load_sem,
     pre_sem,
     edge_sem,
@@ -299,6 +326,7 @@
     groups = block // LANES
     coarse_rows = coarse_hbm.shape[0]
     halo_rows = halo_hbm.shape[0]
+    window = nodes // 2
 
     def rows_of(i):
         return pl.ds(pl.multiple_of(i * block, block), block)
@@ -315,70 +343,119 @@
         rows = rows_of(i)
         return pltpu.make_async_copy(out_v.at[rows], edge_out.at[rows], out_sem.at[i])
 
+    pairs = [
+        (coarse_hbm, table.at[pl.ds(0, coarse_rows)]),
+        (snd_hbm, snd_ref),
+        (halo_hbm, table.at[pl.ds(coarse_rows, halo_rows)]),
+        (rcv_hbm, rcv_ref),
+        (w2_hbm, w2_v),
+        (b2_hbm, rows_v.at[0]),
+        (gain_hbm, rows_v.at[1]),
+        (shift_hbm, rows_v.at[2]),
+        (nb1_hbm, rows_v.at[3]),
+        (nb2_hbm, rows_v.at[4]),
+        (ngain_hbm, rows_v.at[5]),
+        (nshift_hbm, rows_v.at[6]),
+        (node_hbm, node_v),
+        (nw1_hbm, nw1_v),
+        (nw2_hbm, nw2_v),
+    ]
     loads = [
         pltpu.make_async_copy(source, place, load_sem.at[k])
-        for k, (source, place) in enumerate(
-            [
-                (coarse_hbm, table.at[pl.ds(0, coarse_rows)]),
-                (halo_hbm, table.at[pl.ds(coarse_rows, halo_rows)]),
-                (w2_hbm, w2_v),
-                (node_hbm, node_v),
-                (nw1_hbm, nw1_v),
-                (nw2_hbm, nw2_v),
-            ]
-        )
+        for k, (source, place) in enumerate(pairs)
     ]
-    for load in loads[:2]:
+    early, late = loads[:8], loads[8:]
+    for load in loads[:3]:
         load.start()
     pre_copy(0).start()
-    loads[2].start()
+    for load in loads[3:8]:
+        load.start()
     edge_copy(0).start()
     for i in range(1, blocks):
         pre_copy(i).start()
         edge_copy(i).start()
-    for load in loads[3:]:
+    for load in late:
         load.start()
     total[...] = jnp.zeros_like(total)
-    for load in loads[:3]:
+    for load in early:
         load.wait()
 
-    def one_block(i, carry):
-        pre_copy(i).wait()
-        edge_copy(i).wait()
-        rows = rows_of(i)
+    def first_layer(i, hidden):
         wanted = one_hot_rows(snd_ref, i * groups, groups, nodes, coarse_rows + halo_rows)
-        pre = pre_v[rows, :] + jnp.dot(wanted, table[...], preferred_element_type=F32)
-        hidden = silu(pre).astype(BF16)
-        y = jnp.dot(hidden, w2_v[...], preferred_element_type=F32) + b2_ref[...]
-        new = edge_v[rows, :].astype(F32) + layer_norm(y, gain_ref[...], shift_ref[...])
+        half = pre_v[rows_of(i), :] + jnp.dot(
+            wanted, table[...], preferred_element_type=F32
+        )
+        hidden[...] = silu_of_half(half).astype(BF16)
+
+    def second_layer(i, hidden):
+        y = jnp.dot(hidden[...], w2_v[...], preferred_element_type=F32) + rows_v[0]
+        new = edge_v[rows_of(i), :].astype(F32) + layer_norm(y, rows_v[1], rows_v[2])
         live = []
         for g in range(groups):
             row = rcv_ref[pl.ds(i * groups + g, 1), :]
             live.append(jnp.broadcast_to(row, (LANES, LANES)).T[:, :1])
         live = jnp.concatenate(live, axis=0) < nodes
-        new = jnp.where(live, new, 0.0).astype(BF16)
-        out_v[rows, :] = new
+        out_v[rows_of(i), :] = jnp.where(live, new, 0.0).astype(BF16)
+
+    def arrive(i):
+        pre_copy(i).wait()
+        edge_copy(i).wait()
+
+    arrive(0)
+    first_layer(0, hidden_a)
+
+    def two_blocks(p, carry):
+        i = 2 * p
+        arrive(i + 1)
+        arrive(i + 2)
+        first_layer(i + 1, hidden_b)
+        second_layer(i, hidden_a)
+        first_layer(i + 2, hidden_a)
+        second_layer(i + 1, hidden_b)
         out_copy(i).start()
-        total[...] += jnp.dot(
-            one_hot_columns(rcv_ref, i * groups, groups, nodes),
-            new,
-            preferred_element_type=F32,
-        )
+        out_copy(i + 1).start()
         return carry
 
-    lax.fori_loop(0, blocks, one_block, 0)
-
-    for load in loads[3:]:
+    lax.fori_loop(0, blocks // 2 - 1, two_blocks, 0)
+    arrive(blocks - 1)
+    first_layer(blocks - 1, hidden_b)
+    second_layer(blocks - 2, hidden_a)
+    second_layer(blocks - 1, hidden_b)
+    out_copy(blocks - 2).start()
+    out_copy(blocks - 1).start()
+
+    def sum_block(i, carry):
+        lowest = jnp.min(rcv_ref[pl.ds(i * groups, 1), :])
+        highest = jnp.max(rcv_ref[pl.ds(i * groups + groups - 1, 1), :])
+        for start in range(0, nodes, window):
+
+            @pl.when(jnp.logical_and(lowest < start + window, highest >= start))
+            def _():
+                total[pl.ds(start, window), :] += jnp.dot(
+                    one_hot_columns(rcv_ref, i * groups, groups, start, window),
+                    out_v[rows_of(i), :],
+                    preferred_element_type=F32,
+                )
+
+        return carry
+
+    lax.fori_loop(0, blocks, sum_block, 0)
+
+    for load in late:
         load.wait()
     node = node_v[...]
     both = jnp.concatenate([node, total[...].astype(BF16)], axis=1)
-    pre = jnp.dot(both, nw1_v[...], preferred_element_type=F32) + nb1_ref[...]
-    y = jnp.dot(silu(pre).astype(BF16), nw2_v[...], preferred_element_type=F32) + nb2_ref[...]
-    node_out[...] = (
-        node.astype(F32) + layer_norm(y, ngain_ref[...], nshift_ref[...])
-    ).astype(BF16)
+    half = 0.5 * (jnp.dot(both, nw1_v[...], preferred_element_type=F32) + rows_v[3])
+    y = (
+        jnp.dot(silu_of_half(half).astype(BF16), nw2_v[...], preferred_element_type=F32)
+        + rows_v[4]
+    )
+    new_node[...] = (node.astype(F32) + layer_norm(y, rows_v[5], rows_v[6])).astype(BF16)
+    last = pltpu.make_async_copy(new_node, node_out, load_sem.at[len(loads)])
+    last.start()
     for i in range(blocks):
         out_copy(i).wait()
+    last.wait()
 
 
 def on_device(
@@ -407,7 +484,6 @@
     block = min(512, edges)
     blocks = edges // block
     digits = digits_of(n)
-    vmem = pl.BlockSpec(memory_space=pltpu.VMEM)
     hbm = pl.BlockSpec(memory_space=pl.ANY)
     dma = pltpu.SemaphoreType.DMA
     snd = sender.reshape(edges // LANES, LANES)
@@ -423,16 +499,20 @@
             jax.ShapeDtypeStruct(digits + (COARSE_DEV, width), BF16),
             jax.ShapeDtypeStruct((neighbours, slots, width), BF16),
         ),
-        in_specs=[hbm, hbm, vmem, vmem, vmem, hbm, vmem],
+        in_specs=[hbm] * 7,
         out_specs=(hbm, hbm, hbm),
         scratch_shapes=[
+            pltpu.VMEM(snd.shape, jnp.int32),
+            pltpu.VMEM(rcv.shape, jnp.int32),
+            pltpu.VMEM((neighbours, slots), jnp.int32),
+            pltpu.VMEM((1, width), F32),
             pltpu.VMEM((nodes, width), BF16),
             pltpu.VMEM((2 * width, width), BF16),
             pltpu.VMEM((edges, width), BF16),
             pltpu.VMEM((edges, width), F32),
             pltpu.VMEM((width + 2 * nodes, width), BF16),
             pltpu.VMEM((neighbours, slots, width), BF16),
-            dma((4,)),
+            dma((8,)),
             dma((blocks,)),
             dma((blocks,)),
             dma,
@@ -446,7 +526,7 @@
             dma((neighbours,)),
         ],
         compiler_params=pltpu.CompilerParams(
-            collective_id=0, has_side_effects=True, vmem_limit_bytes=48 * 2**20
+            collective_id=0, has_side_effects=True, vmem_limit_bytes=VMEM_BYTES
         ),
         cost_estimate=pl.CostEstimate(
             flops=2 * edges * (width + 2 * nodes) * width,
@@ -464,24 +544,30 @@
             jax.ShapeDtypeStruct((edges, width), BF16),
             jax.ShapeDtypeStruct((nodes, width), BF16),
         ),
-        in_specs=[hbm] * 5 + [vmem] * 2 + [hbm] + [vmem] * 3 + [hbm, vmem, hbm] + [vmem] * 3,
-        out_specs=(hbm, vmem),
+        in_specs=[hbm] * 17,
+        out_specs=(hbm, hbm),
         scratch_shapes=[
             pltpu.VMEM((edges, width), F32),
             pltpu.VMEM((edges, width), BF16),
             pltpu.VMEM((edges, width), BF16),
             pltpu.VMEM((coarse_rows + halo_rows, width), BF16),
+            pltpu.VMEM(snd.shape, jnp.int32),
+            pltpu.VMEM(rcv.shape, jnp.int32),
+            pltpu.VMEM(edge_w2.shape, BF16),
+            pltpu.VMEM((7, 1, width), F32),
             pltpu.VMEM((nodes, width), BF16),
-            pltpu.VMEM(edge_w2.shape, BF16),
             pltpu.VMEM(node_w1.shape, BF16),
             pltpu.VMEM(node_w2.shape, BF16),
             pltpu.VMEM((nodes, width), F32),
-            dma((6,)),
+            pltpu.VMEM((block, width), BF16),
+            pltpu.VMEM((block, width), BF16),
+            pltpu.VMEM((nodes, width), BF16),
+            dma((16,)),
             dma((blocks,)),
             dma((blocks,)),
             dma((blocks,)),
         ],
-        compiler_params=pltpu.CompilerParams(vmem_limit_bytes=48 * 2**20),
+        compiler_params=pltpu.CompilerParams(vmem_limit_bytes=VMEM_BYTES),
         cost_estimate=pl.CostEstimate(
             flops=2 * edges * (2 * width + coarse_rows + halo_rows) * width,
             bytes_accessed=8 * edges * width,

time: 45.6 us -> 38.5 us (0.84); the launches traced: 45.2 us -> 38.7 us
  local copies, waits for them, and re-layouts: 5.28 us -> 0 us
  Pallas kernels: 39.1 us -> 38 us
    unnamed x32 -> x0, local copies, waits for them, and re-layouts: 5.28 us -> none
    pallas_call x1, Pallas kernels: 18.2 us -> 16.9 us  [on_device(): pl.pallas_call(functools.partial(update_kernel, block), out_shape=(jax.Sh...]
where the time goes in v2:
time: 38.5 us; the launch traced here: 38.7 us
  Pallas kernels  38 us (99%)
  between operations  0.64 us (2%)
    pallas_call x1, Pallas kernels, on_device(): pl.pallas_call(functools.partial(exchange_kernel, n, block), out_shape=(j...  21.1 us
    pallas_call x1, Pallas kernels, on_device(): pl.pallas_call(functools.partial(update_kernel, block), out_shape=(jax.Sh...  16.9 us

profile of v2, /device:TPU:0, one launch (start us, length us, event | category | flops | bytes accessed | tf_op | source)
XLA Modules:
  0.0 38.7 jit_solution(11955691364471276649)
XLA Ops:
  0.6 21.1 %exchange.1 = (f32[4096,512]{1,0:T(8,128)}, bf16[4,4,2,16,512]{4,3,2,1,0:T(8,128)(2,1)}, bf16[8,32,512]{2,1,0:T(8,128)(2,1)}) custom-call(bf16[512,512]{1,0:T(8,128)(2,1)} %node_hbm.3, bf16[4096,512]{1,0:T(8,128)(2,1)} %edge_hbm.3, s32[32,128]{1,0:T(8,128)} %bitcast.13, s32[32,128]{1,0:T(8,128)} %bitcast.15, s32[8,32]{1,0:T(8,128)} %bitcast.17, ...), custom_call_target="tpu_custom_call" | custom-call | flops 6442450944 | bytes 12582912 | tf_op jit(solution)/shard_map/exchange/pallas_call | solution.py:495
  21.7 16.9 %update.1 = (bf16[4096,512]{1,0:T(8,128)(2,1)}, bf16[512,512]{1,0:T(8,128)(2,1)}) custom-call(f32[4096,512]{1,0:T(8,128)} %get-tuple-element.5.pre_hbm, bf16[4096,512]{1,0:T(8,128)(2,1)} %edge_hbm.3, bf16[512,512]{1,0:T(8,128)(2,1)} %bitcast.26, bf16[256,512]{1,0:T(8,128)(2,1)} %bitcast.27, bf16[512,512]{1,0:T(8,128)(2,1)} %node_hbm.3, s32[32,128]{1,0:T(8,128)} %bitcast.14, ...), custom_call_target="tpu_custom_call" | custom-call | flops 7516192768 | bytes 16777216 | tf_op jit(solution)/shard_map/update/pallas_call | solution.py:541
